TPU v7x, 32 devices: a whole 2x2x4 slice. The times are simulated.
32 devices in a mesh: groups: 2 (over y), pipe: 4 (over z), hour: 2 (over x), seg: 2 (over core).
Axes of the slice: x: 2, y: 2, z: 4, core: 2. Of those that a mesh axis runs over, the one named last changes fastest.
Arguments:
- segment_flow: float32 [16, 64, 1024], P(('groups', 'hour'), 'seg', 'pipe'), parts along dimension 0, may hold values from -4 to 4
- linepack: float32 [16, 64, 1024], P(('groups', 'hour'), 'seg', 'pipe'), parts along dimension 0, may hold values from 0.2 to 2.4
- mass_dual: float32 [16, 64, 1024], P(('groups', 'hour'), 'seg', 'pipe'), parts along dimension 0, may hold values from -3 to 3
- momentum_dual: float32 [16, 64, 1024], P(('groups', 'hour'), 'seg', 'pipe'), parts along dimension 0, may hold values from -3 to 3
- contract_dual: float32 [16, 2, 32, 128], P(('groups', 'hour'), 'seg', 'pipe'), parts along dimension 0, may hold values from -3 to 3
- flow_cost: float32 [16, 64, 1024], P(('groups', 'hour'), 'seg', 'pipe'), parts along dimension 0, may hold values from -24 to 24
- injection: float32 [16, 64, 1024], P(('groups', 'hour'), 'seg', 'pipe'), parts along dimension 0, may hold values from -3 to 3
- contract_target: float32 [16, 2, 32, 128], P(('groups', 'hour'), 'seg', 'pipe'), parts along dimension 0, may hold values from 0.4 to 2
- friction_table: float32 [16], replicated, may hold values from 0.3 to 3
- friction_class: int32 [64, 2048], P('seg', ('groups', 'pipe')), parts along dimension 1, may hold values from 0 to 15
- matching: int32 [2048], P('groups'), parts along dimension 0, may hold values from 0 to 1023, as said below
- contract_map: int32 [16, 1024], P(('groups', 'hour')), parts along dimension 0, may hold values from 0 to 127
Outputs:
- flow_final: float32 [16, 64, 1024], P(('groups', 'hour'), 'seg', 'pipe'), parts along dimension 0
- linepack_final: float32 [16, 64, 1024], P(('groups', 'hour'), 'seg', 'pipe'), parts along dimension 0
- mass_dual_final: float32 [16, 64, 1024], P(('groups', 'hour'), 'seg', 'pipe'), parts along dimension 0
- momentum_dual_final: float32 [16, 64, 1024], P(('groups', 'hour'), 'seg', 'pipe'), parts along dimension 0
- contract_dual_final: float32 [16, 2, 32, 128], P(('groups', 'hour'), 'seg', 'pipe'), parts along dimension 0
- primal_weight: float32 [2], P('groups'), parts along dimension 0
There are 2 independent parts, one for each index of `groups`. A program takes and returns all parts, laid end to end along the dimension named above; an argument that names none is the same for every part. Nothing has to cross between parts.
Inputs may be any that keep to these rules, and one draw needn't show every extreme that they name: `matching`: every pipe's inlet is fed by the outlet of exactly one pipe: each number of 0 to 1023 appears once; for any two blocks of 256 consecutive pipes, exactly 64 pipes of the first are fed from outlets of the second.
All inputs are finite; a program needn't handle non-finite values.
Results may differ from a plain program's by a relative error of at most 0.0001.
Values sent between devices are 32-bit elements; how exact they have to be, the bound alone decides.
A program may use at most 64 MiB of HBM per device.

v0:
```python
import math
import jax
import jax.numpy as jnp
from jax import lax
from jax.sharding import PartitionSpec as P

ITERS = 2
FLOW_CAP = 1.5
PACK_CAP = 2.5
STEP_SCALE = 0.25
NORM_EPS = 1e-06


def padded(cells, sides, width):
    for axis, dim in sides:
        count = lax.axis_size(axis)
        ends = count - 1
        head = lax.slice_in_dim(cells, 0, width, axis=dim)
        tail = lax.slice_in_dim(cells, cells.shape[dim] - width, cells.shape[dim], axis=dim)
        cells = jnp.concatenate(
            [
                lax.ppermute(tail, axis, [(i, (i + 1) % count) for i in range(ends)]),
                cells,
                lax.ppermute(head, axis, [((i + 1) % count, i) for i in range(ends)]),
            ],
            axis=dim,
        )
    return cells


def widened_pair(stacked):
    return padded(stacked, (("hour", 1), ("seg", 2)), 1)


def other_half(edge_row, half_index, partner_local):
    gathered = lax.all_gather(edge_row[:, None, :], ("pipe", "seg"), axis=1, tiled=True)
    hour_rows, row_count, row_width = gathered.shape
    seg_count = lax.axis_size("seg")
    picked = gathered.reshape(hour_rows, row_count // seg_count, seg_count, row_width)[
        :, :, half_index, :
    ]
    far_rows = picked.reshape(hour_rows, row_count // seg_count * row_width)
    return jnp.take(far_rows, partner_local, axis=1)


def contract_local(values, contract_rows, class_count):
    hour_rows, seg_rows, pipe_rows = values.shape
    block = math.gcd(pipe_rows, 2048)
    classes = jnp.arange(class_count, dtype=jnp.int32)

    def add_block(block_index, total):
        partial_value = lax.dynamic_slice_in_dim(values, block_index * block, block, 2)
        row_map = lax.dynamic_slice_in_dim(contract_rows, block_index * block, block, 1)
        onehot = (row_map[:, :, None] == classes[None, None, :]).astype(jnp.float32)
        return total + jnp.einsum(
            "hsp,hpc->hsc",
            partial_value,
            onehot,
            precision=lax.Precision.HIGHEST,
            preferred_element_type=jnp.float32,
        )

    return lax.fori_loop(
        0, pipe_rows // block, add_block, jnp.zeros((hour_rows, seg_rows, class_count), jnp.float32)
    )


def spread_local(duals, contract_rows):
    hour_rows, seg_rows, class_count = duals.shape
    pipe_rows = contract_rows.shape[1]
    block = math.gcd(pipe_rows, 2048)
    classes = jnp.arange(class_count, dtype=jnp.int32)

    def fill_block(block_index, result_now):
        row_map = lax.dynamic_slice_in_dim(contract_rows, block_index * block, block, 1)
        onehot = (row_map[:, :, None] == classes[None, None, :]).astype(jnp.float32)
        partial_value = jnp.einsum(
            "hsc,hpc->hsp",
            duals,
            onehot,
            precision=lax.Precision.HIGHEST,
            preferred_element_type=jnp.float32,
        )
        return lax.dynamic_update_slice_in_dim(result_now, partial_value, block_index * block, 2)

    return lax.fori_loop(
        0, pipe_rows // block, fill_block, jnp.zeros((hour_rows, seg_rows, pipe_rows), jnp.float32)
    )


def on_device(
    segment_flow,
    linepack,
    mass_dual,
    momentum_dual,
    contract_dual,
    flow_cost,
    injection,
    contract_target,
    friction_table,
    friction_class,
    matching,
    contract_map,
):
    hour_rows, seg_rows, pipe_rows = segment_flow.shape
    class_count = contract_dual.shape[3]
    pipe_count = lax.axis_size("pipe")
    total_pipes = pipe_rows * pipe_count
    share_scale = class_count / total_pipes
    pipe_start = lax.axis_index("pipe") * pipe_rows
    seg_index = lax.axis_index("seg")
    at_start = seg_index == 0
    at_end = seg_index == lax.axis_size("seg") - 1
    levels = jnp.arange(friction_table.shape[0], dtype=jnp.int32)
    friction = jnp.sum(
        jnp.where(
            friction_class[None] == levels[:, None, None], friction_table[:, None, None], 0.0
        ),
        axis=0,
    )[None]
    inverse = (
        jnp.zeros_like(matching).at[matching].set(jnp.arange(matching.shape[0], dtype=jnp.int32))
    )
    source_local = lax.dynamic_slice_in_dim(matching, pipe_start, pipe_rows)
    target_local = lax.dynamic_slice_in_dim(inverse, pipe_start, pipe_rows)
    contract_now = contract_dual.reshape(hour_rows, contract_dual.shape[2], class_count)
    target_now = contract_target.reshape(hour_rows, contract_target.shape[2], class_count)
    weight = jnp.float32(1.0)
    for iteration in range(ITERS):
        primal_step = STEP_SCALE / weight
        dual_step = STEP_SCALE * weight
        widened = widened_pair(jnp.stack([mass_dual, momentum_dual]))
        last_base = widened[0, 1:-1, -1, :]
        later_hour = widened[0, 2:, 1:-1, :]
        before_seg = widened[1, 1:-1, :-2, :]
        returned = other_half(mass_dual[:, 0, :], 0, target_local)
        last_row = last_base + jnp.where(at_end, returned, 0.0)
        next_seg = jnp.concatenate([mass_dual[:, 1:, :], last_row[:, None, :]], axis=1)
        grad_flow = mass_dual - next_seg + friction * momentum_dual
        hour_spread = spread_local(contract_now, contract_map)
        spread = lax.all_to_all(hour_spread, "pipe", split_axis=2, concat_axis=1, tiled=True)
        grad_pack = mass_dual - later_hour - momentum_dual + before_seg + share_scale * spread
        grad_flow, grad_pack = (grad_flow, grad_pack)
        flow_next = jnp.clip(
            segment_flow - primal_step * (flow_cost - grad_flow), -FLOW_CAP, FLOW_CAP
        )
        pack_next = jnp.clip(linepack + primal_step * grad_pack, 0.0, PACK_CAP)
        flow_bar = 2.0 * flow_next - segment_flow
        pack_bar = 2.0 * pack_next - linepack
        forward_widened = widened_pair(jnp.stack([flow_bar, pack_bar]))
        first_base = forward_widened[0, 1:-1, 0, :]
        earlier = forward_widened[1, :-2, 1:-1, :]
        after_seg = forward_widened[1, 1:-1, 2:, :]
        inflow = other_half(flow_bar[:, -1, :], 1, source_local)
        first_row = first_base + jnp.where(at_start, inflow, 0.0)
        upstream = jnp.concatenate([first_row[:, None, :], flow_bar[:, :-1, :]], axis=1)
        mass_rows = pack_bar - earlier + flow_bar - upstream
        momentum = friction * flow_bar - (pack_bar - after_seg)
        hour_major = lax.all_to_all(pack_bar, "pipe", split_axis=1, concat_axis=2, tiled=True)
        totals = contract_local(hour_major, contract_map, class_count)
        mass_rows, momentum, totals = (mass_rows, momentum, share_scale * totals)
        mass_next = mass_dual + dual_step * (injection - mass_rows)
        momentum_next = momentum_dual - dual_step * momentum
        contract_next = contract_now + dual_step * (target_now - totals)
        primal_sq = jnp.sum((flow_next - segment_flow) ** 2) + jnp.sum((pack_next - linepack) ** 2)
        dual_sq = (
            jnp.sum((mass_next - mass_dual) ** 2)
            + jnp.sum((momentum_next - momentum_dual) ** 2)
            + jnp.sum((contract_next - contract_now) ** 2)
        )
        primal_total, dual_total = lax.psum((primal_sq, dual_sq), ("pipe", "hour", "seg"))
        weight = jnp.sqrt(weight * jnp.sqrt((dual_total + NORM_EPS) / (primal_total + NORM_EPS)))
        segment_flow, linepack = (flow_next, pack_next)
        mass_dual, momentum_dual, contract_now = (mass_next, momentum_next, contract_next)
    return (
        segment_flow,
        linepack,
        mass_dual,
        momentum_dual,
        contract_now.reshape(contract_dual.shape),
        weight.reshape(1),
    )


def solution(mesh):
    return jax.shard_map(
        on_device,
        mesh=mesh,
        in_specs=(
            P(("groups", "hour"), "seg", "pipe"),
            P(("groups", "hour"), "seg", "pipe"),
            P(("groups", "hour"), "seg", "pipe"),
            P(("groups", "hour"), "seg", "pipe"),
            P(("groups", "hour"), "seg", "pipe", None),
            P(("groups", "hour"), "seg", "pipe"),
            P(("groups", "hour"), "seg", "pipe"),
            P(("groups", "hour"), "seg", "pipe", None),
            P(),
            P("seg", ("groups", "pipe")),
            P("groups"),
            P(("groups", "hour"), None),
        ),
        out_specs=(
            P(("groups", "hour"), "seg", "pipe"),
            P(("groups", "hour"), "seg", "pipe"),
            P(("groups", "hour"), "seg", "pipe"),
            P(("groups", "hour"), "seg", "pipe"),
            P(("groups", "hour"), "seg", "pipe", None),
            P("groups"),
        ),
        check_vma=False,
    )
```

profile of v0, /device:TPU:0, one launch (start us, length us, event | category | flops | bytes accessed | tf_op | source)
XLA Modules:
  0.0 255.9 jit_solution(9958504613072737630)
XLA Ops:
  0.6 2.2 fusion.4
  3.7 3.1 %reshape.116 = f32[4,1,8192]{2,1,0:T(1,128)} reshape(f32[1024,4,8]{2,1,0:T(4,128)S(1)} %bitcast.195) | data formatting | bytes 262144
  6.8 6.3 %all-to-all-start = ((f32[4,1,8192]{2,1,0:T(1,128)}), f32[4,1,8192]{2,1,0:T(1,128)S(1)}, u32[]{:S(2)}, u32[]{:S(2)}) async-start(f32[4,1,8192]{2,1,0:T(1,128)} %reshape.116), calls=%async_computation | async-start | bytes 262144 | tf_op jit(solution)/shard_map/all_to_all | solution.py:141
  14.5 4.5 %collective-permute-start = (f32[2,1,32,256]{3,2,1,0:T(8,128)S(1)}, f32[2,1,32,256]{3,2,1,0:T(8,128)S(1)}, u32[]{:S(2)}, u32[]{:S(2)}) collective-permute-start(f32[2,1,32,256]{3,2,1,0:T(8,128)S(1)} %get-tuple-element.135), channel_id=1, source_target_pairs={{0,2},{1,3},{4,6},{5,7},{8,10},{9,11},{12,14},{13,15},{16,18},{17,... | collective-permute-start | bytes 196616 | tf_op jit(solution)/shard_map/ppermute | solution.py:22
  19.1 14.6 %all_gather.12 = f32[4,8,256]{2,0,1:T(4,128)S(1)} all-gather(f32[4,1,256]{2,0,1:T(4,128)S(1)} %copy.255), channel_id=1, replica_groups=mesh['groups'=2,'pipe'=4,'hour'=2,'seg'=2] {'pipe','seg'}, dimensions={1}, use_global_device_ids=true | all-gather | bytes 36864 | tf_op jit(solution)/shard_map/all_gather | solution.py:36
  33.9 4.3 %scatter_custom_fusion = s32[1024]{0:T(1024)S(1)} fusion(s32[1024]{0:T(1024)S(1)} %compare_select_fusion, s32[1024]{0:T(1024)S(1)} %iota.14, s32[]{:T(128)} %constant.26.clone.1), kind=kCustom, calls=%fused_computation.140 | custom fusion | bytes 4100 | tf_op jit(solution)/shard_map/scatter | solution.py:122
  40.3 2.2 collective-permute-start.3
  47.8 2.5 reshape.117
  50.4 1.8 broadcast_multiply_fusion.1
  52.2 1.9 copy.145
  58.7 4.5 %collective-permute-start.4 = (f32[2,1,32,256]{3,2,1,0:T(8,128)S(1)}, f32[2,1,32,256]{3,2,1,0:T(8,128)S(1)}, u32[]{:S(2)}, u32[]{:S(2)}) collective-permute-start(f32[2,1,32,256]{3,2,1,0:T(8,128)S(1)} %get-tuple-element.131), channel_id=1, source_target_pairs={{0,2},{1,3},{4,6},{5,7},{8,10},{9,11},{12,14},{13,15},{16,18},{17,... | collective-permute-start | bytes 196616 | tf_op jit(solution)/shard_map/ppermute | solution.py:22
  63.3 14.0 %all_gather.13 = f32[4,8,256]{2,0,1:T(4,128)S(1)} all-gather(f32[4,1,256]{2,0,1:T(4,128)S(1)} %slice.182), channel_id=1, replica_groups=mesh['groups'=2,'pipe'=4,'hour'=2,'seg'=2] {'pipe','seg'}, dimensions={1}, use_global_device_ids=true | all-gather | bytes 36864 | tf_op jit(solution)/shard_map/all_gather | solution.py:36
  78.7 2.2 collective-permute-start.6
  84.0 2.0 multiply_reduce_fusion.7
  87.5 4.5 %collective-permute-start.8 = (f32[2,1,32,256]{3,2,1,0:T(8,128)S(1)}, f32[2,1,32,256]{3,2,1,0:T(8,128)S(1)}, u32[]{:S(2)}, u32[]{:S(2)}) collective-permute-start(f32[2,1,32,256]{3,2,1,0:T(8,128)S(1)} %get-tuple-element.127), channel_id=1, source_target_pairs={{0,2},{1,3},{4,6},{5,7},{8,10},{9,11},{12,14},{13,15},{16,18},{17,... | collective-permute-start | bytes 196616 | tf_op jit(solution)/shard_map/ppermute | solution.py:22
  92.0 4.5 %all-to-all-start.1 = ((f32[4,32,256]{2,0,1:T(4,128)}), f32[4,32,256]{2,0,1:T(4,128)S(1)}, u32[]{:S(2)}, u32[]{:S(2)}) async-start(f32[4,32,256]{2,0,1:T(4,128)} %multiply_subtract_fusion.3), calls=%async_computation.1 | async-start | bytes 262144 | tf_op jit(solution)/shard_map/all_to_all | solution.py:159
  98.5 14.6 %all_gather.14 = f32[4,8,256]{2,0,1:T(4,128)S(1)} all-gather(f32[4,1,256]{2,0,1:T(4,128)S(1)} %slice.191), channel_id=1, replica_groups=mesh['groups'=2,'pipe'=4,'hour'=2,'seg'=2] {'pipe','seg'}, dimensions={1}, use_global_device_ids=true | all-gather | bytes 36864 | tf_op jit(solution)/shard_map/all_gather | solution.py:36
  116.3 2.2 collective-permute-start.11
  120.7 2.2 fusion.73
  122.9 1.8 fusion.1
  125.6 3.1 %reshape.118 = f32[4,1,8192]{2,1,0:T(1,128)} reshape(f32[1024,4,8]{2,1,0:T(4,128)S(1)} %bitcast.197) | data formatting | bytes 262144
  128.7 4.5 %all-to-all-start.2 = ((f32[4,1,8192]{2,1,0:T(1,128)}), f32[4,1,8192]{2,1,0:T(1,128)S(1)}, u32[]{:S(2)}, u32[]{:S(2)}) async-start(f32[4,1,8192]{2,1,0:T(1,128)} %reshape.118), calls=%async_computation.2 | async-start | bytes 262144 | tf_op jit(solution)/shard_map/all_to_all | solution.py:141
  135.1 33.5 %all-reduce.1 = (f32[]{:T(128)}, f32[]{:T(128)}) all-reduce(f32[]{:T(128)S(6)} %add.153, f32[]{:T(128)S(6)} %add.155), channel_id=1, replica_groups=mesh['groups'=2,'pipe'=4,'hour'=2,'seg'=2] {'pipe','hour','seg'}, use_global_device_ids=true, to_apply=%region_5.7 | all-reduce | flops 2 | bytes 16 | tf_op jit(solution)/shard_map/psum | solution.py:171
  171.0 2.5 reshape.119
  175.4 1.9 copy.175
  181.3 4.5 %collective-permute-start.12 = (f32[2,1,32,256]{3,2,1,0:T(8,128)S(1)}, f32[2,1,32,256]{3,2,1,0:T(8,128)S(1)}, u32[]{:S(2)}, u32[]{:S(2)}) collective-permute-start(f32[2,1,32,256]{3,2,1,0:T(8,128)S(1)} %get-tuple-element.123), channel_id=1, source_target_pairs={{0,2},{1,3},{4,6},{5,7},{8,10},{9,11},{12,14},{13,15},{16,18},{17,... | collective-permute-start | bytes 196616 | tf_op jit(solution)/shard_map/ppermute | solution.py:22
  187.2 3.5 %all-to-all-start.3 = ((f32[4,32,256]{2,0,1:T(4,128)}), f32[4,32,256]{2,0,1:T(4,128)S(1)}, u32[]{:S(2)}, u32[]{:S(2)}) async-start(f32[4,32,256]{2,0,1:T(4,128)} %multiply_subtract_fusion.1), calls=%async_computation.3 | async-start | bytes 262144 | tf_op jit(solution)/shard_map/all_to_all | solution.py:159
  190.7 14.6 %all_gather.15 = f32[4,8,256]{2,0,1:T(4,128)S(1)} all-gather(f32[4,1,256]{2,0,1:T(4,128)S(1)} %slice.198), channel_id=1, replica_groups=mesh['groups'=2,'pipe'=4,'hour'=2,'seg'=2] {'pipe','seg'}, dimensions={1}, use_global_device_ids=true | all-gather | bytes 36864 | tf_op jit(solution)/shard_map/all_gather | solution.py:36
  209.4 3.0 %collective-permute-start.14 = (f32[2,6,1,256]{1,3,2,0:T(8,128)S(1)}, f32[2,6,1,256]{1,3,2,0:T(8,128)S(1)}, u32[]{:S(2)}, u32[]{:S(2)}) collective-permute-start(f32[2,6,1,256]{1,3,2,0:T(8,128)S(1)} %copy.201), channel_id=1, source_target_pairs={{0,1},{2,3},{4,5},{6,7},{8,9},{10,11},{12,13},{14,15},{16,17},{18,... | collective-permute-start | bytes 36872 | tf_op jit(solution)/shard_map/ppermute | solution.py:22
  213.8 1.8 multiply_reduce_fusion.2
  217.6 2.4 multiply_reduce_fusion.8
  221.4 32.0 %all-reduce = (f32[]{:T(128)}, f32[]{:T(128)}) all-reduce(f32[]{:T(128)S(6)} %add.167, f32[]{:T(128)S(6)} %add.169), channel_id=1, replica_groups=mesh['groups'=2,'pipe'=4,'hour'=2,'seg'=2] {'pipe','hour','seg'}, use_global_device_ids=true, to_apply=%region_12.14 | all-reduce | flops 2 | bytes 16 | tf_op jit(solution)/shard_map/psum | solution.py:171
  (151 shorter events, 40.3 us)
Async XLA Ops:
  2.8 10.3 %copy-start = (f32[4,32,256]{2,1,0:T(8,128)S(1)}, f32[4,32,256]{2,1,0:T(8,128)}, u32[]{:S(2)}) copy-start(f32[4,32,256]{2,1,0:T(8,128)} %param.16) | copy-start | bytes 393220
  2.8 10.3 %copy-start.1 = (f32[4,32,256]{2,1,0:T(8,128)S(1)}, f32[4,32,256]{2,1,0:T(8,128)}, u32[]{:S(2)}) copy-start(f32[4,32,256]{2,1,0:T(8,128)} %param.17) | copy-start | bytes 393220
  3.7 30.2 %copy-start.12 = (s32[1024]{0:T(1024)S(1)}, s32[1024]{0:T(1024)}, u32[]{:S(2)}) copy-start(s32[1024]{0:T(1024)} %param.24) | copy-start | bytes 12292
  3.7 35.3 %copy-start.11 = (s32[32,256]{1,0:T(8,128)S(1)}, s32[32,256]{1,0:T(8,128)}, u32[]{:S(2)}) copy-start(s32[32,256]{1,0:T(8,128)} %param.23) | copy-start | bytes 98308
  3.7 35.3 %copy-start.13 = (f32[16]{0:T(128)S(1)}, f32[16]{0:T(128)}, u32[]{:S(2)}) copy-start(f32[16]{0:T(128)} %param.22) | copy-start | bytes 196
  6.8 39.5 %all-to-all-start = ((f32[4,1,8192]{2,1,0:T(1,128)}), f32[4,1,8192]{2,1,0:T(1,128)S(1)}, u32[]{:S(2)}, u32[]{:S(2)}) async-start(f32[4,1,8192]{2,1,0:T(1,128)} %reshape.116), calls=%async_computation | async-start | bytes 262144 | tf_op jit(solution)/shard_map/all_to_all | solution.py:141
  13.2 26.8 %collective-permute-start.1 = (f32[2,1,32,256]{3,2,1,0:T(8,128)S(1)}, f32[2,1,32,256]{3,2,1,0:T(8,128)S(1)}, u32[]{:S(2)}, u32[]{:S(2)}) collective-permute-start(f32[2,1,32,256]{3,2,1,0:T(8,128)S(1)} %get-tuple-element.136), channel_id=1, source_target_pairs={{2,0},{3,1},{6,4},{7,5},{10,8},{11,9},{14,12},{15,13},{18,16},{19,... | collective-permute-start | bytes 196616 | tf_op jit(solution)/shard_map/ppermute | solution.py:24
  14.5 25.5 %collective-permute-start = (f32[2,1,32,256]{3,2,1,0:T(8,128)S(1)}, f32[2,1,32,256]{3,2,1,0:T(8,128)S(1)}, u32[]{:S(2)}, u32[]{:S(2)}) collective-permute-start(f32[2,1,32,256]{3,2,1,0:T(8,128)S(1)} %get-tuple-element.135), channel_id=1, source_target_pairs={{0,2},{1,3},{4,6},{5,7},{8,10},{9,11},{12,14},{13,15},{16,18},{17,... | collective-permute-start | bytes 196616 | tf_op jit(solution)/shard_map/ppermute | solution.py:22
  40.3 13.8 %collective-permute-start.3 = (f32[2,6,1,256]{3,1,2,0:T(8,128)S(1)}, f32[2,6,1,256]{3,1,2,0:T(8,128)S(1)}, u32[]{:S(2)}, u32[]{:S(2)}) collective-permute-start(f32[2,6,1,256]{3,1,2,0:T(8,128)S(1)} %slice.177), channel_id=1, source_target_pairs={{0,1},{2,3},{4,5},{6,7},{8,9},{10,11},{12,13},{14,15},{16,17},{18,... | collective-permute-start | bytes 36872 | tf_op jit(solution)/shard_map/ppermute | solution.py:22
  42.7 3.4 %collective-permute-start.2 = (f32[2,6,1,256]{1,3,2,0:T(8,128)S(1)}, f32[2,6,1,256]{1,3,2,0:T(8,128)S(1)}, u32[]{:S(2)}, u32[]{:S(2)}) collective-permute-start(f32[2,6,1,256]{1,3,2,0:T(8,128)S(1)} %copy.191), channel_id=1, source_target_pairs={{1,0},{3,2},{5,4},{7,6},{9,8},{11,10},{13,12},{15,14},{17,16},{19,... | collective-permute-start | bytes 36872 | tf_op jit(solution)/shard_map/ppermute | solution.py:24
  52.2 2.0 copy-start.8
  52.2 2.0 copy-start.9
  57.2 26.8 %copy-start.6 = (f32[4,32,256]{2,1,0:T(8,128)S(1)}, f32[4,32,256]{2,1,0:T(8,128)}, u32[]{:S(2)}) copy-start(f32[4,32,256]{2,1,0:T(8,128)} %param.20) | copy-start | bytes 393220
  57.2 21.0 %collective-permute-start.5 = (f32[2,1,32,256]{3,2,1,0:T(8,128)S(1)}, f32[2,1,32,256]{3,2,1,0:T(8,128)S(1)}, u32[]{:S(2)}, u32[]{:S(2)}) collective-permute-start(f32[2,1,32,256]{3,2,1,0:T(8,128)S(1)} %get-tuple-element.132), channel_id=1, source_target_pairs={{2,0},{3,1},{6,4},{7,5},{10,8},{11,9},{14,12},{15,13},{18,16},{19,... | collective-permute-start | bytes 196616 | tf_op jit(solution)/shard_map/ppermute | solution.py:24
  58.7 19.6 %collective-permute-start.4 = (f32[2,1,32,256]{3,2,1,0:T(8,128)S(1)}, f32[2,1,32,256]{3,2,1,0:T(8,128)S(1)}, u32[]{:S(2)}, u32[]{:S(2)}) collective-permute-start(f32[2,1,32,256]{3,2,1,0:T(8,128)S(1)} %get-tuple-element.131), channel_id=1, source_target_pairs={{0,2},{1,3},{4,6},{5,7},{8,10},{9,11},{12,14},{13,15},{16,18},{17,... | collective-permute-start | bytes 196616 | tf_op jit(solution)/shard_map/ppermute | solution.py:22
  78.7 3.7 %collective-permute-start.6 = (f32[2,6,1,256]{1,3,2,0:T(8,128)S(1)}, f32[2,6,1,256]{1,3,2,0:T(8,128)S(1)}, u32[]{:S(2)}, u32[]{:S(2)}) collective-permute-start(f32[2,6,1,256]{1,3,2,0:T(8,128)S(1)} %copy.195), channel_id=1, source_target_pairs={{0,1},{2,3},{4,5},{6,7},{8,9},{10,11},{12,13},{14,15},{16,17},{18,... | collective-permute-start | bytes 36872 | tf_op jit(solution)/shard_map/ppermute | solution.py:22
  81.0 3.1 %collective-permute-start.7 = (f32[2,6,1,256]{3,1,2,0:T(8,128)S(1)}, f32[2,6,1,256]{3,1,2,0:T(8,128)S(1)}, u32[]{:S(2)}, u32[]{:S(2)}) collective-permute-start(f32[2,6,1,256]{3,1,2,0:T(8,128)S(1)} %slice.185), channel_id=1, source_target_pairs={{1,0},{3,2},{5,4},{7,6},{9,8},{11,10},{13,12},{15,14},{17,16},{19,... | collective-permute-start | bytes 36872 | tf_op jit(solution)/shard_map/ppermute | solution.py:24
  86.1 34.6 %copy-start.14 = (f32[4,1,8,128]{3,2,1,0:T(8,128)S(1)}, f32[4,1,8,128]{3,2,1,0:T(8,128)}, u32[]{:S(2)}) copy-start(f32[4,1,8,128]{3,2,1,0:T(8,128)} %param.18) | copy-start | bytes 49156
  86.1 34.6 %copy-start.15 = (s32[4,1024]{1,0:T(4,128)S(1)}, s32[4,1024]{1,0:T(4,128)}, u32[]{:S(2)}) copy-start(s32[4,1024]{1,0:T(4,128)} %param.25) | copy-start | bytes 49156
  86.1 34.6 %copy-start.16 = (f32[4,1,8,128]{3,2,1,0:T(8,128)S(1)}, f32[4,1,8,128]{3,2,1,0:T(8,128)}, u32[]{:S(2)}) copy-start(f32[4,1,8,128]{3,2,1,0:T(8,128)} %param.21) | copy-start | bytes 49156
  86.2 29.8 %collective-permute-start.9 = (f32[2,1,32,256]{3,2,1,0:T(8,128)S(1)}, f32[2,1,32,256]{3,2,1,0:T(8,128)S(1)}, u32[]{:S(2)}, u32[]{:S(2)}) collective-permute-start(f32[2,1,32,256]{3,2,1,0:T(8,128)S(1)} %get-tuple-element.128), channel_id=1, source_target_pairs={{2,0},{3,1},{6,4},{7,5},{10,8},{11,9},{14,12},{15,13},{18,16},{19,... | collective-permute-start | bytes 196616 | tf_op jit(solution)/shard_map/ppermute | solution.py:24
  87.5 28.5 %collective-permute-start.8 = (f32[2,1,32,256]{3,2,1,0:T(8,128)S(1)}, f32[2,1,32,256]{3,2,1,0:T(8,128)S(1)}, u32[]{:S(2)}, u32[]{:S(2)}) collective-permute-start(f32[2,1,32,256]{3,2,1,0:T(8,128)S(1)} %get-tuple-element.127), channel_id=1, source_target_pairs={{0,2},{1,3},{4,6},{5,7},{8,10},{9,11},{12,14},{13,15},{16,18},{17,... | collective-permute-start | bytes 196616 | tf_op jit(solution)/shard_map/ppermute | solution.py:22
  92.0 28.6 %all-to-all-start.1 = ((f32[4,32,256]{2,0,1:T(4,128)}), f32[4,32,256]{2,0,1:T(4,128)S(1)}, u32[]{:S(2)}, u32[]{:S(2)}) async-start(f32[4,32,256]{2,0,1:T(4,128)} %multiply_subtract_fusion.3), calls=%async_computation.1 | async-start | bytes 262144 | tf_op jit(solution)/shard_map/all_to_all | solution.py:159
  116.3 61.0 %collective-permute-start.11 = (f32[2,6,1,256]{3,1,2,0:T(8,128)S(1)}, f32[2,6,1,256]{3,1,2,0:T(8,128)S(1)}, u32[]{:S(2)}, u32[]{:S(2)}) collective-permute-start(f32[2,6,1,256]{3,1,2,0:T(8,128)S(1)} %slice.193), channel_id=1, source_target_pairs={{0,1},{2,3},{4,5},{6,7},{8,9},{10,11},{12,13},{14,15},{16,17},{18,... | collective-permute-start | bytes 36872 | tf_op jit(solution)/shard_map/ppermute | solution.py:22
  119.3 13.9 %collective-permute-start.10 = (f32[2,6,1,256]{1,3,2,0:T(8,128)}, f32[2,6,1,256]{1,3,2,0:T(8,128)}, u32[]{:S(2)}, u32[]{:S(2)}) collective-permute-start(f32[2,6,1,256]{1,3,2,0:T(8,128)} %copy.197), channel_id=1, source_target_pairs={{1,0},{3,2},{5,4},{7,6},{9,8},{11,10},{13,12},{15,14},{17,16},{19,... | collective-permute-start | bytes 36872 | tf_op jit(solution)/shard_map/ppermute | solution.py:24
  128.7 41.3 %all-to-all-start.2 = ((f32[4,1,8192]{2,1,0:T(1,128)}), f32[4,1,8192]{2,1,0:T(1,128)S(1)}, u32[]{:S(2)}, u32[]{:S(2)}) async-start(f32[4,1,8192]{2,1,0:T(1,128)} %reshape.118), calls=%async_computation.2 | async-start | bytes 262144 | tf_op jit(solution)/shard_map/all_to_all | solution.py:141
  180.0 27.6 %collective-permute-start.13 = (f32[2,1,32,256]{3,2,1,0:T(8,128)S(1)}, f32[2,1,32,256]{3,2,1,0:T(8,128)S(1)}, u32[]{:S(2)}, u32[]{:S(2)}) collective-permute-start(f32[2,1,32,256]{3,2,1,0:T(8,128)S(1)} %get-tuple-element.124), channel_id=1, source_target_pairs={{2,0},{3,1},{6,4},{7,5},{10,8},{11,9},{14,12},{15,13},{18,16},{19,... | collective-permute-start | bytes 196616 | tf_op jit(solution)/shard_map/ppermute | solution.py:24
  181.3 26.3 %collective-permute-start.12 = (f32[2,1,32,256]{3,2,1,0:T(8,128)S(1)}, f32[2,1,32,256]{3,2,1,0:T(8,128)S(1)}, u32[]{:S(2)}, u32[]{:S(2)}) collective-permute-start(f32[2,1,32,256]{3,2,1,0:T(8,128)S(1)} %get-tuple-element.123), channel_id=1, source_target_pairs={{0,2},{1,3},{4,6},{5,7},{8,10},{9,11},{12,14},{13,15},{16,18},{17,... | collective-permute-start | bytes 196616 | tf_op jit(solution)/shard_map/ppermute | solution.py:22
  187.2 26.6 %copy-start.7 = (f32[4,32,256]{2,1,0:T(8,128)S(1)}, f32[4,32,256]{2,1,0:T(8,128)}, u32[]{:S(2)}) copy-start(f32[4,32,256]{2,1,0:T(8,128)} %param.20) | copy-start | bytes 393220
  187.2 30.4 %all-to-all-start.3 = ((f32[4,32,256]{2,0,1:T(4,128)}), f32[4,32,256]{2,0,1:T(4,128)S(1)}, u32[]{:S(2)}, u32[]{:S(2)}) async-start(f32[4,32,256]{2,0,1:T(4,128)} %multiply_subtract_fusion.1), calls=%async_computation.3 | async-start | bytes 262144 | tf_op jit(solution)/shard_map/all_to_all | solution.py:159
  207.9 5.8 %collective-permute-start.15 = (f32[2,6,1,256]{3,1,2,0:T(8,128)S(1)}, f32[2,6,1,256]{3,1,2,0:T(8,128)S(1)}, u32[]{:S(2)}, u32[]{:S(2)}) collective-permute-start(f32[2,6,1,256]{3,1,2,0:T(8,128)S(1)} %slice.201), channel_id=1, source_target_pairs={{1,0},{3,2},{5,4},{7,6},{9,8},{11,10},{13,12},{15,14},{17,16},{19,... | collective-permute-start | bytes 36872 | tf_op jit(solution)/shard_map/ppermute | solution.py:24
  209.4 4.2 %collective-permute-start.14 = (f32[2,6,1,256]{1,3,2,0:T(8,128)S(1)}, f32[2,6,1,256]{1,3,2,0:T(8,128)S(1)}, u32[]{:S(2)}, u32[]{:S(2)}) collective-permute-start(f32[2,6,1,256]{1,3,2,0:T(8,128)S(1)} %copy.201), channel_id=1, source_target_pairs={{0,1},{2,3},{4,5},{6,7},{8,9},{10,11},{12,13},{14,15},{16,17},{18,... | collective-permute-start | bytes 36872 | tf_op jit(solution)/shard_map/ppermute | solution.py:22
  (5 other events, 9.7 us)
where the time goes:
time: 257 us; the launch traced here: 256 us
  blocking collectives  123 us (48%)
  starting transfers between devices  57.3 us (22%)
  local copies, waits for them, and re-layouts  34.9 us (14%)
  other arithmetic  15.8 us (6%)
  between operations  12.1 us (5%)
  matrix products  8.66 us (3%)
  waiting for transfers between devices  3.97 us (2%)
    psum x2, blocking collectives, on_device(): lax.psum((primal_sq, dual_sq), ('pipe', 'hour', 'seg'))  65.5 us
    all_gather x4, blocking collectives, other_half(): lax.all_gather(edge_row[:, None, :], ('pipe', 'seg'), axis=1, tiled=True)  57.8 us
    ppermute x8, starting transfers between devices, padded(): lax.ppermute(tail, axis, [(i, (i + 1) % count) for i in range(ends)])  27.9 us
    unnamed x55, local copies, waits for them, and re-layouts  17 us
    all_to_all x2, starting transfers between devices, on_device(): lax.all_to_all(hour_spread, 'pipe', split_axis=2, concat_axis=1, tiled=True)  10.8 us
    ppermute x8, starting transfers between devices, padded(): lax.ppermute(head, axis, [((i + 1) % count, i) for i in range(ends)])  10.6 us
    all_to_all x2, starting transfers between devices, on_device(): lax.all_to_all(pack_bar, 'pipe', split_axis=1, concat_axis=2, tiled=True)  7.96 us
  transfers between devices with their start and end apart: 20, of which 3 were waited for; matrix products, arithmetic and copies ran while one was open for 16% of the time, Pallas kernels for 0%

commit v1 on v0

--- a/solution.py
+++ b/solution.py
@@ -168,7 +168,7 @@
             + jnp.sum((momentum_next - momentum_dual) ** 2)
             + jnp.sum((contract_next - contract_now) ** 2)
         )
-        primal_total, dual_total = lax.psum((primal_sq, dual_sq), ("pipe", "hour", "seg"))
+        primal_total, dual_total = lax.psum(lax.psum((primal_sq, dual_sq), ("hour", "seg")), "pipe")
         weight = jnp.sqrt(weight * jnp.sqrt((dual_total + NORM_EPS) / (primal_total + NORM_EPS)))
         segment_flow, linepack = (flow_next, pack_next)
         mass_dual, momentum_dual, contract_now = (mass_next, momentum_next, contract_next)

time: 257 us -> 231 us (0.90)
  blocking collectives: 123 us -> 96.6 us
    psum x2 -> x4, blocking collectives: 65.5 us -> 38.8 us  [the longest x2 24.6 us: on_device(): lax.psum(lax.psum((primal_sq, dual_sq), ('hour', 'seg')), 'pipe')]
  transfers between devices with their start and end apart: 20 -> 20, of which waited for: 3 -> 3; matrix products, arithmetic and copies ran while one was open for 16% -> 18% of each run, Pallas kernels for 0% -> 0%
where the time goes in v1:
time: 231 us; the launch traced here: 229 us
  blocking collectives  96.6 us (42%)
  starting transfers between devices  57.3 us (25%)
  local copies, waits for them, and re-layouts  35.1 us (15%)
  other arithmetic  15.6 us (7%)
  between operations  11.9 us (5%)
  matrix products  8.93 us (4%)
  waiting for transfers between devices  3.97 us (2%)
    all_gather x4, blocking collectives, other_half(): lax.all_gather(edge_row[:, None, :], ('pipe', 'seg'), axis=1, tiled=True)  57.8 us
    ppermute x8, starting transfers between devices, padded(): lax.ppermute(tail, axis, [(i, (i + 1) % count) for i in range(ends)])  27.9 us
    psum x2, blocking collectives, on_device(): lax.psum(lax.psum((primal_sq, dual_sq), ('hour', 'seg')), 'pipe')  24.6 us
    unnamed x55, local copies, waits for them, and re-layouts  17 us
    psum x2, blocking collectives, on_device(): lax.psum((primal_sq, dual_sq), ('hour', 'seg'))  14.2 us
    all_to_all x2, starting transfers between devices, on_device(): lax.all_to_all(hour_spread, 'pipe', split_axis=2, concat_axis=1, tiled=True)  10.8 us
    ppermute x8, starting transfers between devices, padded(): lax.ppermute(head, axis, [((i + 1) % count, i) for i in range(ends)])  10.6 us
    all_to_all x2, starting transfers between devices, on_device(): lax.all_to_all(pack_bar, 'pipe', split_axis=1, concat_axis=2, tiled=True)  7.96 us
  transfers between devices with their start and end apart: 20, of which 3 were waited for; matrix products, arithmetic and copies ran while one was open for 18% of the time, Pallas kernels for 0%

profile of v1, /device:TPU:0, one launch (start us, length us, event | category | flops | bytes accessed | tf_op | source)
XLA Modules:
  0.0 229.4 jit_solution(2815113595825467222)
XLA Ops:
  0.6 2.2 fusion.4
  3.7 3.1 %reshape.116 = f32[4,1,8192]{2,1,0:T(1,128)} reshape(f32[1024,4,8]{2,1,0:T(4,128)S(1)} %bitcast.195) | data formatting | bytes 262144
  6.8 6.3 %all-to-all-start = ((f32[4,1,8192]{2,1,0:T(1,128)}), f32[4,1,8192]{2,1,0:T(1,128)S(1)}, u32[]{:S(2)}, u32[]{:S(2)}) async-start(f32[4,1,8192]{2,1,0:T(1,128)} %reshape.116), calls=%async_computation | async-start | bytes 262144 | tf_op jit(solution)/shard_map/all_to_all | solution.py:141
  14.5 4.5 %collective-permute-start = (f32[2,1,32,256]{3,2,1,0:T(8,128)S(1)}, f32[2,1,32,256]{3,2,1,0:T(8,128)S(1)}, u32[]{:S(2)}, u32[]{:S(2)}) collective-permute-start(f32[2,1,32,256]{3,2,1,0:T(8,128)S(1)} %get-tuple-element.139), channel_id=1, source_target_pairs={{0,2},{1,3},{4,6},{5,7},{8,10},{9,11},{12,14},{13,15},{16,18},{17,... | collective-permute-start | bytes 196616 | tf_op jit(solution)/shard_map/ppermute | solution.py:22
  19.1 14.6 %all_gather.12 = f32[4,8,256]{2,0,1:T(4,128)S(1)} all-gather(f32[4,1,256]{2,0,1:T(4,128)S(1)} %copy.255), channel_id=1, replica_groups=mesh['groups'=2,'pipe'=4,'hour'=2,'seg'=2] {'pipe','seg'}, dimensions={1}, use_global_device_ids=true | all-gather | bytes 36864 | tf_op jit(solution)/shard_map/all_gather | solution.py:36
  33.9 4.3 %scatter_custom_fusion = s32[1024]{0:T(1024)S(1)} fusion(s32[1024]{0:T(1024)S(1)} %compare_select_fusion, s32[1024]{0:T(1024)S(1)} %iota.14, s32[]{:T(128)} %constant.26.clone.1), kind=kCustom, calls=%fused_computation.140 | custom fusion | bytes 4100 | tf_op jit(solution)/shard_map/scatter | solution.py:122
  40.3 2.2 collective-permute-start.3
  47.8 2.5 %reshape.117 = f32[1024,4,8]{2,1,0:T(4,128)S(1)} reshape(f32[4,8192]{1,0:T(4,128)S(1)} %reduce) | data formatting | bytes 262144
  52.2 1.9 copy.145
  58.6 4.5 %collective-permute-start.4 = (f32[2,1,32,256]{3,2,1,0:T(8,128)S(1)}, f32[2,1,32,256]{3,2,1,0:T(8,128)S(1)}, u32[]{:S(2)}, u32[]{:S(2)}) collective-permute-start(f32[2,1,32,256]{3,2,1,0:T(8,128)S(1)} %get-tuple-element.135), channel_id=1, source_target_pairs={{0,2},{1,3},{4,6},{5,7},{8,10},{9,11},{12,14},{13,15},{16,18},{17,... | collective-permute-start | bytes 196616 | tf_op jit(solution)/shard_map/ppermute | solution.py:22
  63.2 14.0 %all_gather.13 = f32[4,8,256]{2,0,1:T(4,128)S(1)} all-gather(f32[4,1,256]{2,0,1:T(4,128)S(1)} %slice.182), channel_id=1, replica_groups=mesh['groups'=2,'pipe'=4,'hour'=2,'seg'=2] {'pipe','seg'}, dimensions={1}, use_global_device_ids=true | all-gather | bytes 36864 | tf_op jit(solution)/shard_map/all_gather | solution.py:36
  78.7 2.2 collective-permute-start.6
  84.0 1.9 multiply_reduce_fusion.7
  87.4 4.5 %collective-permute-start.8 = (f32[2,1,32,256]{3,2,1,0:T(8,128)S(1)}, f32[2,1,32,256]{3,2,1,0:T(8,128)S(1)}, u32[]{:S(2)}, u32[]{:S(2)}) collective-permute-start(f32[2,1,32,256]{3,2,1,0:T(8,128)S(1)} %get-tuple-element.131), channel_id=1, source_target_pairs={{0,2},{1,3},{4,6},{5,7},{8,10},{9,11},{12,14},{13,15},{16,18},{17,... | collective-permute-start | bytes 196616 | tf_op jit(solution)/shard_map/ppermute | solution.py:22
  91.9 4.5 %all-to-all-start.1 = ((f32[4,32,256]{2,0,1:T(4,128)}), f32[4,32,256]{2,0,1:T(4,128)S(1)}, u32[]{:S(2)}, u32[]{:S(2)}) async-start(f32[4,32,256]{2,0,1:T(4,128)} %multiply_subtract_fusion.3), calls=%async_computation.1 | async-start | bytes 262144 | tf_op jit(solution)/shard_map/all_to_all | solution.py:159
  98.4 14.6 %all_gather.14 = f32[4,8,256]{2,0,1:T(4,128)S(1)} all-gather(f32[4,1,256]{2,0,1:T(4,128)S(1)} %slice.191), channel_id=1, replica_groups=mesh['groups'=2,'pipe'=4,'hour'=2,'seg'=2] {'pipe','seg'}, dimensions={1}, use_global_device_ids=true | all-gather | bytes 36864 | tf_op jit(solution)/shard_map/all_gather | solution.py:36
  115.6 2.2 collective-permute-start.11
  120.0 2.2 fusion.73
  122.2 2.1 fusion.1
  126.0 3.1 %reshape.118 = f32[4,1,8192]{2,1,0:T(1,128)} reshape(f32[1024,4,8]{2,1,0:T(4,128)S(1)} %bitcast.197) | data formatting | bytes 262144
  129.0 4.5 %all-to-all-start.2 = ((f32[4,1,8192]{2,1,0:T(1,128)}), f32[4,1,8192]{2,1,0:T(1,128)S(1)}, u32[]{:S(2)}, u32[]{:S(2)}) async-start(f32[4,1,8192]{2,1,0:T(1,128)} %reshape.118), calls=%async_computation.2 | async-start | bytes 262144 | tf_op jit(solution)/shard_map/all_to_all | solution.py:141
  135.3 7.7 %all-reduce.1 = (f32[]{:T(128)}, f32[]{:T(128)}) all-reduce(f32[]{:T(128)S(6)} %add.161, f32[]{:T(128)S(6)} %add.163), channel_id=1, replica_groups=mesh['groups'=2,'pipe'=4,'hour'=2,'seg'=2] {'hour','seg'}, use_global_device_ids=true, to_apply=%region_5.7 | all-reduce | flops 2 | bytes 16 | tf_op jit(solution)/shard_map/psum | solution.py:171
  143.0 12.5 %all-reduce.3 = (f32[]{:T(128)}, f32[]{:T(128)}) all-reduce(f32[]{:T(128)} %get-tuple-element.99, f32[]{:T(128)} %get-tuple-element.100), channel_id=1, replica_groups=mesh['groups'=2,'pipe'=4,'hour'=2,'seg'=2] {'pipe'}, use_global_device_ids=true, to_apply=%region_6.8 | all-reduce | flops 2 | bytes 16 | tf_op jit(solution)/shard_map/psum | solution.py:171
  158.0 2.5 %reshape.119 = f32[1024,4,8]{2,1,0:T(4,128)S(1)} reshape(f32[4,8192]{1,0:T(4,128)S(1)} %reduce.1) | data formatting | bytes 262144
  162.3 1.9 copy.175
  168.2 4.5 %collective-permute-start.12 = (f32[2,1,32,256]{3,2,1,0:T(8,128)S(1)}, f32[2,1,32,256]{3,2,1,0:T(8,128)S(1)}, u32[]{:S(2)}, u32[]{:S(2)}) collective-permute-start(f32[2,1,32,256]{3,2,1,0:T(8,128)S(1)} %get-tuple-element.127), channel_id=1, source_target_pairs={{0,2},{1,3},{4,6},{5,7},{8,10},{9,11},{12,14},{13,15},{16,18},{17,... | collective-permute-start | bytes 196616 | tf_op jit(solution)/shard_map/ppermute | solution.py:22
  174.1 3.5 %all-to-all-start.3 = ((f32[4,32,256]{2,0,1:T(4,128)}), f32[4,32,256]{2,0,1:T(4,128)S(1)}, u32[]{:S(2)}, u32[]{:S(2)}) async-start(f32[4,32,256]{2,0,1:T(4,128)} %multiply_subtract_fusion.1), calls=%async_computation.3 | async-start | bytes 262144 | tf_op jit(solution)/shard_map/all_to_all | solution.py:159
  177.6 14.6 %all_gather.15 = f32[4,8,256]{2,0,1:T(4,128)S(1)} all-gather(f32[4,1,256]{2,0,1:T(4,128)S(1)} %slice.198), channel_id=1, replica_groups=mesh['groups'=2,'pipe'=4,'hour'=2,'seg'=2] {'pipe','seg'}, dimensions={1}, use_global_device_ids=true | all-gather | bytes 36864 | tf_op jit(solution)/shard_map/all_gather | solution.py:36
  196.3 3.0 %collective-permute-start.14 = (f32[2,6,1,256]{1,3,2,0:T(8,128)S(1)}, f32[2,6,1,256]{1,3,2,0:T(8,128)S(1)}, u32[]{:S(2)}, u32[]{:S(2)}) collective-permute-start(f32[2,6,1,256]{1,3,2,0:T(8,128)S(1)} %copy.201), channel_id=1, source_target_pairs={{0,1},{2,3},{4,5},{6,7},{8,9},{10,11},{12,13},{14,15},{16,17},{18,... | collective-permute-start | bytes 36872 | tf_op jit(solution)/shard_map/ppermute | solution.py:22
  204.6 2.4 %multiply_reduce_fusion.8 = (f32[]{:T(128)}, f32[4,8,128]{2,1,0:T(8,128)}) fusion(f32[4,8,128]{2,1,0:T(8,128)S(1)} %get-tuple-element.142, f32[4,8,1024]{2,1,0:T(8,128)S(1)} %bitcast.215, s32[4,1024]{1,0:T(4,128)S(1)} %copy-done.15, f32[4,1,8,128]{3,2,1,0:T(8,128)S(1)} %copy-done.16, f32[]{:T(128)S(6)} %mul.158), kind=kOutput, calls=%fused_computation.134 | convolution fusion | flops 50884608 | bytes 196616 | tf_op jit(solution)/shard_map/while/body/eval_jaxpr/hsp,hpc->hsc/dot_general | solution.py:55
  208.3 6.5 %all-reduce = (f32[]{:T(128)}, f32[]{:T(128)}) all-reduce(f32[]{:T(128)S(6)} %add.175, f32[]{:T(128)S(6)} %add.177), channel_id=1, replica_groups=mesh['groups'=2,'pipe'=4,'hour'=2,'seg'=2] {'hour','seg'}, use_global_device_ids=true, to_apply=%region_14.16 | all-reduce | flops 2 | bytes 16 | tf_op jit(solution)/shard_map/psum | solution.py:171
  214.8 12.1 %all-reduce.2 = (f32[]{:T(128)}, f32[]{:T(128)}) all-reduce(f32[]{:T(128)} %get-tuple-element.97, f32[]{:T(128)} %get-tuple-element.98), channel_id=1, replica_groups=mesh['groups'=2,'pipe'=4,'hour'=2,'seg'=2] {'pipe'}, use_global_device_ids=true, to_apply=%region_15.17 | all-reduce | flops 2 | bytes 16 | tf_op jit(solution)/shard_map/psum | solution.py:171
  (153 shorter events, 44.0 us)
Async XLA Ops:
  2.8 10.3 %copy-start = (f32[4,32,256]{2,1,0:T(8,128)S(1)}, f32[4,32,256]{2,1,0:T(8,128)}, u32[]{:S(2)}) copy-start(f32[4,32,256]{2,1,0:T(8,128)} %param.16) | copy-start | bytes 393220
  2.8 10.3 %copy-start.1 = (f32[4,32,256]{2,1,0:T(8,128)S(1)}, f32[4,32,256]{2,1,0:T(8,128)}, u32[]{:S(2)}) copy-start(f32[4,32,256]{2,1,0:T(8,128)} %param.17) | copy-start | bytes 393220
  3.7 30.2 %copy-start.12 = (s32[1024]{0:T(1024)S(1)}, s32[1024]{0:T(1024)}, u32[]{:S(2)}) copy-start(s32[1024]{0:T(1024)} %param.24) | copy-start | bytes 12292
  3.7 35.3 %copy-start.11 = (s32[32,256]{1,0:T(8,128)S(1)}, s32[32,256]{1,0:T(8,128)}, u32[]{:S(2)}) copy-start(s32[32,256]{1,0:T(8,128)} %param.23) | copy-start | bytes 98308
  3.7 35.3 %copy-start.13 = (f32[16]{0:T(128)S(1)}, f32[16]{0:T(128)}, u32[]{:S(2)}) copy-start(f32[16]{0:T(128)} %param.22) | copy-start | bytes 196
  6.8 39.5 %all-to-all-start = ((f32[4,1,8192]{2,1,0:T(1,128)}), f32[4,1,8192]{2,1,0:T(1,128)S(1)}, u32[]{:S(2)}, u32[]{:S(2)}) async-start(f32[4,1,8192]{2,1,0:T(1,128)} %reshape.116), calls=%async_computation | async-start | bytes 262144 | tf_op jit(solution)/shard_map/all_to_all | solution.py:141
  13.2 26.8 %collective-permute-start.1 = (f32[2,1,32,256]{3,2,1,0:T(8,128)S(1)}, f32[2,1,32,256]{3,2,1,0:T(8,128)S(1)}, u32[]{:S(2)}, u32[]{:S(2)}) collective-permute-start(f32[2,1,32,256]{3,2,1,0:T(8,128)S(1)} %get-tuple-element.140), channel_id=1, source_target_pairs={{2,0},{3,1},{6,4},{7,5},{10,8},{11,9},{14,12},{15,13},{18,16},{19,... | collective-permute-start | bytes 196616 | tf_op jit(solution)/shard_map/ppermute | solution.py:24
  14.5 25.5 %collective-permute-start = (f32[2,1,32,256]{3,2,1,0:T(8,128)S(1)}, f32[2,1,32,256]{3,2,1,0:T(8,128)S(1)}, u32[]{:S(2)}, u32[]{:S(2)}) collective-permute-start(f32[2,1,32,256]{3,2,1,0:T(8,128)S(1)} %get-tuple-element.139), channel_id=1, source_target_pairs={{0,2},{1,3},{4,6},{5,7},{8,10},{9,11},{12,14},{13,15},{16,18},{17,... | collective-permute-start | bytes 196616 | tf_op jit(solution)/shard_map/ppermute | solution.py:22
  40.3 13.8 %collective-permute-start.3 = (f32[2,6,1,256]{3,1,2,0:T(8,128)S(1)}, f32[2,6,1,256]{3,1,2,0:T(8,128)S(1)}, u32[]{:S(2)}, u32[]{:S(2)}) collective-permute-start(f32[2,6,1,256]{3,1,2,0:T(8,128)S(1)} %slice.177), channel_id=1, source_target_pairs={{0,1},{2,3},{4,5},{6,7},{8,9},{10,11},{12,13},{14,15},{16,17},{18,... | collective-permute-start | bytes 36872 | tf_op jit(solution)/shard_map/ppermute | solution.py:22
  42.7 3.4 %collective-permute-start.2 = (f32[2,6,1,256]{1,3,2,0:T(8,128)S(1)}, f32[2,6,1,256]{1,3,2,0:T(8,128)S(1)}, u32[]{:S(2)}, u32[]{:S(2)}) collective-permute-start(f32[2,6,1,256]{1,3,2,0:T(8,128)S(1)} %copy.191), channel_id=1, source_target_pairs={{1,0},{3,2},{5,4},{7,6},{9,8},{11,10},{13,12},{15,14},{17,16},{19,... | collective-permute-start | bytes 36872 | tf_op jit(solution)/shard_map/ppermute | solution.py:24
  52.1 2.0 copy-start.8
  52.1 2.0 copy-start.9
  57.2 26.8 %copy-start.6 = (f32[4,32,256]{2,1,0:T(8,128)S(1)}, f32[4,32,256]{2,1,0:T(8,128)}, u32[]{:S(2)}) copy-start(f32[4,32,256]{2,1,0:T(8,128)} %param.20) | copy-start | bytes 393220
  57.2 21.0 %collective-permute-start.5 = (f32[2,1,32,256]{3,2,1,0:T(8,128)S(1)}, f32[2,1,32,256]{3,2,1,0:T(8,128)S(1)}, u32[]{:S(2)}, u32[]{:S(2)}) collective-permute-start(f32[2,1,32,256]{3,2,1,0:T(8,128)S(1)} %get-tuple-element.136), channel_id=1, source_target_pairs={{2,0},{3,1},{6,4},{7,5},{10,8},{11,9},{14,12},{15,13},{18,16},{19,... | collective-permute-start | bytes 196616 | tf_op jit(solution)/shard_map/ppermute | solution.py:24
  58.6 19.6 %collective-permute-start.4 = (f32[2,1,32,256]{3,2,1,0:T(8,128)S(1)}, f32[2,1,32,256]{3,2,1,0:T(8,128)S(1)}, u32[]{:S(2)}, u32[]{:S(2)}) collective-permute-start(f32[2,1,32,256]{3,2,1,0:T(8,128)S(1)} %get-tuple-element.135), channel_id=1, source_target_pairs={{0,2},{1,3},{4,6},{5,7},{8,10},{9,11},{12,14},{13,15},{16,18},{17,... | collective-permute-start | bytes 196616 | tf_op jit(solution)/shard_map/ppermute | solution.py:22
  78.7 3.7 %collective-permute-start.6 = (f32[2,6,1,256]{1,3,2,0:T(8,128)S(1)}, f32[2,6,1,256]{1,3,2,0:T(8,128)S(1)}, u32[]{:S(2)}, u32[]{:S(2)}) collective-permute-start(f32[2,6,1,256]{1,3,2,0:T(8,128)S(1)} %copy.195), channel_id=1, source_target_pairs={{0,1},{2,3},{4,5},{6,7},{8,9},{10,11},{12,13},{14,15},{16,17},{18,... | collective-permute-start | bytes 36872 | tf_op jit(solution)/shard_map/ppermute | solution.py:22
  80.9 3.1 %collective-permute-start.7 = (f32[2,6,1,256]{3,1,2,0:T(8,128)S(1)}, f32[2,6,1,256]{3,1,2,0:T(8,128)S(1)}, u32[]{:S(2)}, u32[]{:S(2)}) collective-permute-start(f32[2,6,1,256]{3,1,2,0:T(8,128)S(1)} %slice.185), channel_id=1, source_target_pairs={{1,0},{3,2},{5,4},{7,6},{9,8},{11,10},{13,12},{15,14},{17,16},{19,... | collective-permute-start | bytes 36872 | tf_op jit(solution)/shard_map/ppermute | solution.py:24
  86.0 33.9 %copy-start.14 = (f32[4,1,8,128]{3,2,1,0:T(8,128)S(1)}, f32[4,1,8,128]{3,2,1,0:T(8,128)}, u32[]{:S(2)}) copy-start(f32[4,1,8,128]{3,2,1,0:T(8,128)} %param.18) | copy-start | bytes 49156
  86.0 33.9 %copy-start.15 = (s32[4,1024]{1,0:T(4,128)S(1)}, s32[4,1024]{1,0:T(4,128)}, u32[]{:S(2)}) copy-start(s32[4,1024]{1,0:T(4,128)} %param.25) | copy-start | bytes 49156
  86.1 33.9 %copy-start.16 = (f32[4,1,8,128]{3,2,1,0:T(8,128)S(1)}, f32[4,1,8,128]{3,2,1,0:T(8,128)}, u32[]{:S(2)}) copy-start(f32[4,1,8,128]{3,2,1,0:T(8,128)} %param.21) | copy-start | bytes 49156
  86.1 29.1 %collective-permute-start.9 = (f32[2,1,32,256]{3,2,1,0:T(8,128)S(1)}, f32[2,1,32,256]{3,2,1,0:T(8,128)S(1)}, u32[]{:S(2)}, u32[]{:S(2)}) collective-permute-start(f32[2,1,32,256]{3,2,1,0:T(8,128)S(1)} %get-tuple-element.132), channel_id=1, source_target_pairs={{2,0},{3,1},{6,4},{7,5},{10,8},{11,9},{14,12},{15,13},{18,16},{19,... | collective-permute-start | bytes 196616 | tf_op jit(solution)/shard_map/ppermute | solution.py:24
  87.4 27.9 %collective-permute-start.8 = (f32[2,1,32,256]{3,2,1,0:T(8,128)S(1)}, f32[2,1,32,256]{3,2,1,0:T(8,128)S(1)}, u32[]{:S(2)}, u32[]{:S(2)}) collective-permute-start(f32[2,1,32,256]{3,2,1,0:T(8,128)S(1)} %get-tuple-element.131), channel_id=1, source_target_pairs={{0,2},{1,3},{4,6},{5,7},{8,10},{9,11},{12,14},{13,15},{16,18},{17,... | collective-permute-start | bytes 196616 | tf_op jit(solution)/shard_map/ppermute | solution.py:22
  91.9 28.0 %all-to-all-start.1 = ((f32[4,32,256]{2,0,1:T(4,128)}), f32[4,32,256]{2,0,1:T(4,128)S(1)}, u32[]{:S(2)}, u32[]{:S(2)}) async-start(f32[4,32,256]{2,0,1:T(4,128)} %multiply_subtract_fusion.3), calls=%async_computation.1 | async-start | bytes 262144 | tf_op jit(solution)/shard_map/all_to_all | solution.py:159
  115.6 48.6 %collective-permute-start.11 = (f32[2,6,1,256]{3,1,2,0:T(8,128)S(1)}, f32[2,6,1,256]{3,1,2,0:T(8,128)S(1)}, u32[]{:S(2)}, u32[]{:S(2)}) collective-permute-start(f32[2,6,1,256]{3,1,2,0:T(8,128)S(1)} %slice.193), channel_id=1, source_target_pairs={{0,1},{2,3},{4,5},{6,7},{8,9},{10,11},{12,13},{14,15},{16,17},{18,... | collective-permute-start | bytes 36872 | tf_op jit(solution)/shard_map/ppermute | solution.py:22
  118.6 14.9 %collective-permute-start.10 = (f32[2,6,1,256]{1,3,2,0:T(8,128)}, f32[2,6,1,256]{1,3,2,0:T(8,128)}, u32[]{:S(2)}, u32[]{:S(2)}) collective-permute-start(f32[2,6,1,256]{1,3,2,0:T(8,128)} %copy.197), channel_id=1, source_target_pairs={{1,0},{3,2},{5,4},{7,6},{9,8},{11,10},{13,12},{15,14},{17,16},{19,... | collective-permute-start | bytes 36872 | tf_op jit(solution)/shard_map/ppermute | solution.py:24
  129.0 27.9 %all-to-all-start.2 = ((f32[4,1,8192]{2,1,0:T(1,128)}), f32[4,1,8192]{2,1,0:T(1,128)S(1)}, u32[]{:S(2)}, u32[]{:S(2)}) async-start(f32[4,1,8192]{2,1,0:T(1,128)} %reshape.118), calls=%async_computation.2 | async-start | bytes 262144 | tf_op jit(solution)/shard_map/all_to_all | solution.py:141
  166.9 27.6 %collective-permute-start.13 = (f32[2,1,32,256]{3,2,1,0:T(8,128)S(1)}, f32[2,1,32,256]{3,2,1,0:T(8,128)S(1)}, u32[]{:S(2)}, u32[]{:S(2)}) collective-permute-start(f32[2,1,32,256]{3,2,1,0:T(8,128)S(1)} %get-tuple-element.128), channel_id=1, source_target_pairs={{2,0},{3,1},{6,4},{7,5},{10,8},{11,9},{14,12},{15,13},{18,16},{19,... | collective-permute-start | bytes 196616 | tf_op jit(solution)/shard_map/ppermute | solution.py:24
  168.2 26.3 %collective-permute-start.12 = (f32[2,1,32,256]{3,2,1,0:T(8,128)S(1)}, f32[2,1,32,256]{3,2,1,0:T(8,128)S(1)}, u32[]{:S(2)}, u32[]{:S(2)}) collective-permute-start(f32[2,1,32,256]{3,2,1,0:T(8,128)S(1)} %get-tuple-element.127), channel_id=1, source_target_pairs={{0,2},{1,3},{4,6},{5,7},{8,10},{9,11},{12,14},{13,15},{16,18},{17,... | collective-permute-start | bytes 196616 | tf_op jit(solution)/shard_map/ppermute | solution.py:22
  174.1 26.6 %copy-start.7 = (f32[4,32,256]{2,1,0:T(8,128)S(1)}, f32[4,32,256]{2,1,0:T(8,128)}, u32[]{:S(2)}) copy-start(f32[4,32,256]{2,1,0:T(8,128)} %param.20) | copy-start | bytes 393220
  174.1 30.4 %all-to-all-start.3 = ((f32[4,32,256]{2,0,1:T(4,128)}), f32[4,32,256]{2,0,1:T(4,128)S(1)}, u32[]{:S(2)}, u32[]{:S(2)}) async-start(f32[4,32,256]{2,0,1:T(4,128)} %multiply_subtract_fusion.1), calls=%async_computation.3 | async-start | bytes 262144 | tf_op jit(solution)/shard_map/all_to_all | solution.py:159
  194.8 5.8 %collective-permute-start.15 = (f32[2,6,1,256]{3,1,2,0:T(8,128)S(1)}, f32[2,6,1,256]{3,1,2,0:T(8,128)S(1)}, u32[]{:S(2)}, u32[]{:S(2)}) collective-permute-start(f32[2,6,1,256]{3,1,2,0:T(8,128)S(1)} %slice.201), channel_id=1, source_target_pairs={{1,0},{3,2},{5,4},{7,6},{9,8},{11,10},{13,12},{15,14},{17,16},{19,... | collective-permute-start | bytes 36872 | tf_op jit(solution)/shard_map/ppermute | solution.py:24
  196.3 4.2 %collective-permute-start.14 = (f32[2,6,1,256]{1,3,2,0:T(8,128)S(1)}, f32[2,6,1,256]{1,3,2,0:T(8,128)S(1)}, u32[]{:S(2)}, u32[]{:S(2)}) collective-permute-start(f32[2,6,1,256]{1,3,2,0:T(8,128)S(1)} %copy.201), channel_id=1, source_target_pairs={{0,1},{2,3},{4,5},{6,7},{8,9},{10,11},{12,13},{14,15},{16,17},{18,... | collective-permute-start | bytes 36872 | tf_op jit(solution)/shard_map/ppermute | solution.py:22
  (5 other events, 9.7 us)
